TPU v7x, 32 devices: a whole 2x2x4 slice. The times are simulated.
32 devices in a mesh: lon: 16 (over z, x, core), lat: 2 (over y).
Axes of the slice: x: 2, y: 2, z: 4, core: 2. Of those that a mesh axis runs over, the one named last changes fastest.
Arguments:
- potential_heat: float32 [8, 256, 2048], P(None, 'lat', 'lon'), may hold values from -6 to 6
- saltiness_anomaly: float32 [8, 256, 2048], P(None, 'lat', 'lon'), may hold values from -6 to 6
- east_current: float32 [8, 256, 2048], P(None, 'lat', 'lon'), may hold values from -1 to 1
- north_current: float32 [8, 256, 2048], P(None, 'lat', 'lon'), may hold values from -1 to 1
- water_indicator: int32 [8, 256, 2048], P(None, 'lat', 'lon'), may hold values from 0 to 1, as said below
- east_west_courant_factor: float32 [256, 2048], P('lat', 'lon'), may hold values from 0.05 to 0.45
- north_south_courant_factor: float32 [256, 2048], P('lat', 'lon'), may hold values from 0.05 to 0.45
- interface_diffusion_factor: float32 [7, 256, 2048], P(None, 'lat', 'lon'), may hold values from 0.05 to 5
- spreading_coefficient: float32 [4, 8], replicated, may hold values from 0.05 to 0.25
- seam_mirror_index: int32 [2048], P('lon'), may hold values from 0 to 2047, as said below
Outputs:
- temperature_next: float32 [8, 256, 2048], P(None, 'lat', 'lon')
- salinity_next: float32 [8, 256, 2048], P(None, 'lat', 'lon')
- zonal_next: float32 [8, 256, 2048], P(None, 'lat', 'lon')
- meridional_next: float32 [8, 256, 2048], P(None, 'lat', 'lon')
Inputs may be any that keep to these rules, and one draw needn't show every extreme that they name: water_indicator is 0 or 1, and a cell below a land cell is land. seam_mirror_index[i] = (p - i) mod 2048 for one p whose remainder on division by 128 is 127.
All inputs are finite; a program needn't handle non-finite values.
Results may differ from a plain program's by a relative error of at most 0.0003.
Values sent between devices are 32-bit elements; how exact they have to be, the bound alone decides.
A program may use at most 128 MiB of HBM per device.

v0:
```python
import functools

import jax
import jax.numpy as jnp
from jax import lax
from jax.experimental import pallas as pl
from jax.experimental.pallas import tpu as pltpu
from jax.sharding import PartitionSpec as P

LANES = 128
SP, VM, VMP, WET, WETP, MY, MYP, WX, WXP, PLANES = 32, 34, 42, 43, 51, 52, 53, 54, 62, 63
WIDE, THIN = 34, 20
MSG = WIDE * 4 + THIN * 2
VMEM_LIMIT = 56 * 1024 * 1024


def lane_of(rows):
    return lax.broadcasted_iota(jnp.int32, (rows, LANES), 1)


def roll(x, s):
    if isinstance(s, int):
        s = s % LANES
        if s == 0:
            return x
    return pltpu.roll(x, s, 1)


def shifted(q, halo, s, lane):
    if s > 0:
        return roll(jnp.where(lane < s, halo, q), -s)
    return roll(jnp.where(lane >= LANES + s, halo, q), -s)


def group_roll(x, g):
    return pltpu.roll(x, (LANES - 8 * g) % LANES, 1)


def coefs(courant, opening):
    a = jnp.abs(courant)
    ak = a * (1.0 - (2.0 / 3.0) * a)
    cc = courant * opening
    return (
        cc * (1.0 - 0.5 * a - 1.5 * ak),
        cc * (0.5 * a - 1.5 * ak),
        cc * (3.0 * ak),
        courant >= 0.0,
    )


def edge(qm, q0, q1, q2):
    return (7.0 / 12.0) * (q0 + q1) - (1.0 / 12.0) * (qm + q2)


def flux(cf, em, e0, e1, q0, q1):
    a0, a1, a2, up = cf
    return a0 * e0 + a1 * jnp.where(up, em, e1) + a2 * jnp.where(up, q0, q1)


def pack_array(a, refs, wet_ref, mx_ref, my_ref, c_ref):
    rows = 32
    total = c_ref.shape[1]
    lane = lane_of(rows)
    group = ((lane + 4) % LANES) // 8

    def chunk(i, carry):
        r = pl.ds(pl.multiple_of(i * rows, rows), rows)
        wets = [wet_ref[k, r, :].astype(jnp.float32) for k in range(8)]
        acc = jnp.zeros((rows, LANES), jnp.float32)
        if a < 2:
            items = [refs[2 * a + h][k, r, :] * wets[k] for h in range(2) for k in range(8)]
        else:
            items = wets + [mx_ref[r, :], my_ref[r, :]]
        for g, x in enumerate(items):
            acc = jnp.where(group == g, roll(x, 8 * g), acc)
        c_ref[a, r, :] = acc
        return carry

    lax.fori_loop(0, total // rows, chunk, 0)


def packed_x(c_ref, l_ref, r_ref, T, get, tr, rows):
    lane = lane_of(rows)
    low = lane % 8 < 4
    place = (lane + 4) % LANES
    half = place < 64
    group = place // 8
    parts = []
    for right in (True, False):
        near, far = (c_ref, r_ref) if right else (l_ref, c_ref)
        e = [jnp.where(low, get(far, a), get(near, a)) for a in range(3)]

        def both(x, first):
            y = pltpu.roll(x, 64, 1)
            return jnp.where(half, x, y) if first else jnp.where(half, y, x)

        def spread(x, g):
            x = jnp.where(group == g, x, 0.0)
            for s in (8, 16, 32, 64):
                x = x + pltpu.roll(x, s, 1)
            return x

        u, v, wet = both(e[1], True), both(e[1], False), both(e[2], True)
        mx, my = spread(e[2], 8), spread(e[2], 9)
        um = u * mx
        opening = wet * roll(wet, -1)
        weight = 0.5 * (mx + roll(mx, -1)) * opening
        cf = coefs(0.5 * (um + roll(um, -1)), opening)
        starred, fluxes, edges = [], [], []
        for a in range(2):
            q = e[a]
            q1 = roll(q, -1)
            ed = edge(roll(q, 1), q, q1, roll(q, -2))
            f = flux(cf, roll(ed, 1), ed, roll(ed, -1), q, q1)
            starred.append(q + roll(f, 1) - f)
            fluxes.append(f)
            edges.append(ed)
        parts.append((starred, fluxes, edges, weight, v * my, wet, my))
    (rs, _, re, _, rvm, rwet, rmy), (ls, lf, le, lw, lvm, lwet, lmy) = parts
    for a in range(2):
        T[SP + a, tr, :] = jnp.where(low, rs[a], ls[a])
    T[VMP, tr, :] = jnp.where(low, rvm, lvm)
    T[WETP, tr, :] = jnp.where(low, rwet, lwet)
    T[MYP, tr, :] = jnp.where(low, rmy, lmy)
    T[WXP, tr, :] = lw
    return lf, [jnp.where(low, re[a], le[a]) for a in range(2)]


def x_phase(fields, wet_ref, mx_ref, my_ref, c_ref, l_ref, r_ref, T, H, get, tr, rows, unroll):
    lane = lane_of(rows)
    low = lane % 8 < 4
    lf, le = packed_x(c_ref, l_ref, r_ref, T, get, tr, rows)
    for a in range(3):
        H[a] = jnp.where(low, get(r_ref, a), get(l_ref, a))
    for a in range(2):
        H[3 + a] = lf[a]
        H[5 + a] = le[a]
    mx = get(mx_ref)
    my = get(my_ref)
    T[MY, tr, :] = my
    mxh = group_roll(H[2], 8)
    mx1 = shifted(mx, mxh, 1, lane)

    def level(k, carry):
        wet = get(wet_ref, k).astype(jnp.float32)
        T[WET + k, tr, :] = wet
        hwet = group_roll(H[2], k)
        opening = wet * shifted(wet, hwet, 1, lane)
        T[WX + k, tr, :] = 0.5 * (mx + mx1) * opening
        hu = group_roll(H[1], k)
        um = get(fields[2], k) * wet * mx
        cf = coefs(0.5 * (um + shifted(um, hu * mxh, 1, lane)), opening)
        for f in range(4):
            q = get(fields[f], k) * wet
            if f == 3:
                T[VM + k, tr, :] = q * my
            g = 8 * (f % 2) + k
            h = hu if f == 2 else group_roll(H[f // 2], g)
            qm, q1, q2 = (shifted(q, h, s, lane) for s in (-1, 1, 2))
            ed = edge(qm, q, q1, q2)
            he = group_roll(H[5 + f // 2], g)
            em = roll(jnp.where(lane == LANES - 1, he, ed), 1)
            e1 = roll(jnp.where(lane == 0, he, ed), -1)
            fl = flux(cf, em, ed, e1, q, q1)
            flm = roll(jnp.where(lane == LANES - 1, group_roll(H[3 + f // 2], g), fl), 1)
            T[8 * f + k, tr, :] = q + flm - fl

    def levels(i, carry):
        for j in range(unroll):
            level(i * unroll + j, 0)
        return carry

    lax.fori_loop(0, 8 // unroll, levels, 0)


def face_y(T, vm, wet, my, WY, kw, r0, rows):
    r, r1 = pl.ds(r0, rows), pl.ds(r0 + 1, rows)
    opening = T[wet, r, :] * T[wet, r1, :]
    if WY is not None:
        WY[kw, r, :] = 0.5 * (T[my, r, :] + T[my, r1, :]) * opening
    return coefs(0.5 * (T[vm, r, :] + T[vm, r1, :]), opening)


def y_advect(T, E, F, A, WY, planes, vm, wet, my, kw, chunks):
    for r0, rows in chunks:
        for n, p in enumerate(planes):
            E[n, pl.ds(r0, rows), :] = edge(*(T[p, pl.ds(r0 + s, rows), :] for s in (-1, 0, 1, 2)))
    for r0, rows in chunks:
        cf = face_y(T, vm, wet, my, WY, kw, r0, rows)
        for n, p in enumerate(planes):
            em, e0, e1 = (E[n, pl.ds(r0 + s, rows), :] for s in (-1, 0, 1))
            q0, q1 = (T[p, pl.ds(r0 + s, rows), :] for s in (0, 1))
            F[n, pl.ds(r0, rows), :] = flux(cf, em, e0, e1, q0, q1)
    for r0, rows in chunks:
        for n, p in enumerate(planes):
            r = pl.ds(r0, rows)
            A[p, r, :] = T[p, r, :] + F[n, pl.ds(r0 - 1, rows), :] - F[n, r, :]


def y_phase(T, E, F, A, WY, chunks):
    y_advect(T, E, F, A, None, (SP, SP + 1), VMP, WETP, MYP, 0, chunks)

    def level(k, carry):
        y_advect(T, E, F, A, WY, tuple(8 * f + k for f in range(4)), VM + k, WET + k, MY, k, chunks)
        return carry

    lax.fori_loop(0, 8, level, 0)


def factorize(T, idf_ref, U, INV, FAC, base, rows):
    r = pl.ds(base, rows)
    wet = T[WET, r, :]
    up, factor = None, None
    for k in range(8):
        divisor = 1.0
        if k > 0:
            divisor = divisor + up * (1.0 - factor)
        if k < 7:
            below = T[WET + k + 1, r, :]
            down = idf_ref[k] * wet * below
            wet = below
            U[k] = down
            divisor = divisor + down
        inv = 1.0 / divisor
        INV[k] = inv
        if k < 7:
            factor = down * inv
            FAC[k] = factor
            up = down


def finish(T, A, WY, U, INV, FAC, coef_ref, outs, t0, o0, rows):
    lane = lane_of(rows)
    r, rp, rm = pl.ds(t0, rows), pl.ds(t0 + 1, rows), pl.ds(t0 - 1, rows)
    o = pl.ds(o0, rows)
    wxp = T[WXP, r, :]
    ap = [A[SP + a, r, :] for a in range(2)]
    reduced = []
    for k in range(8):
        wx = T[WX + k, r, :]
        wxm = roll(jnp.where(lane == LANES - 1, roll(wxp, -8 * k), wx), 1)
        wy, wym = WY[k, r, :], WY[k, rm, :]
        inv = INV[k, o, :]
        row = []
        for f in range(4):
            p = 8 * f + k
            a = A[p, r, :]
            h = roll(ap[f // 2], -8 * (8 * (f % 2) + k))
            a1 = roll(jnp.where(lane == 0, h, a), -1)
            am = roll(jnp.where(lane == LANES - 1, h, a), 1)
            lap = wx * (a1 - a) - wxm * (a - am) + wy * (A[p, rp, :] - a) - wym * (a - A[p, rm, :])
            d = a + coef_ref[f, k] * lap
            if k > 0:
                d = d + U[k - 1, o, :] * reduced[-1][f]
            row.append(d * inv)
        reduced.append(row)
    x = reduced[7]
    for k in range(7, -1, -1):
        if k < 7:
            factor = FAC[k, o, :]
            x = [reduced[k][f] + factor * x[f] for f in range(4)]
        wet = T[WET + k, r, :]
        for f in range(4):
            outs[f][k, o, :] = x[f] * wet


LOW = 4
MESH = pl.DeviceIdType.MESH


def halo_kernel(
    lon_n, lat_n, tile, t, s, u, v, wet, mx, my, c_out, l_out, r_out, south, north,
    C, L, R, T, H, Mn, Ms, FS, FN, RA, RB, back,
    s_lon, r_lon, s_lat, r_lat, s_a, r_a, s_b, r_b,
):
    total = t.shape[1]
    me = lax.axis_index("lon")
    lat = lax.axis_index("lat")
    right, left = lax.rem(me + 1, lon_n), lax.rem(me + lon_n - 1, lon_n)
    low, high = lax.rem(me, LOW), me // LOW
    layers = lon_n // LOW
    first, last = lat == 0, lat == lat_n - 1
    ring = [left, right]
    ring += [high * LOW + lax.rem(low + d, LOW) for d in range(1, LOW)]
    ring += [lax.rem(high + d, layers) * LOW + low for d in range(1, layers)]
    barrier = pltpu.get_barrier_semaphore()
    for other in ring:
        pl.semaphore_signal(barrier, inc=1, device_id={"lon": other}, device_id_type=MESH)

    @pl.when(jnp.logical_not(first))
    def _():
        pl.semaphore_signal(barrier, inc=1, device_id={"lat": lat - 1}, device_id_type=MESH)

    @pl.when(jnp.logical_not(last))
    def _():
        pl.semaphore_signal(barrier, inc=1, device_id={"lat": lat + 1}, device_id_type=MESH)

    def send(src, dst, ss, rs, where):
        return pltpu.make_async_remote_copy(
            src_ref=src, dst_ref=dst, send_sem=ss, recv_sem=rs, device_id=where, device_id_type=MESH
        )

    fields = (t, s, u, v)
    lon_copies = []
    for a in range(3):
        pack_array(a, fields, wet, mx, my, C)
        if a == 0:
            peers = len(ring) + jnp.where(first, 0, 1) + jnp.where(last, 0, 1)
            pl.semaphore_wait(barrier, peers)
        for dst, where, i in ((R, left, 0), (L, right, 1)):
            cp = send(C.at[a], dst.at[a], s_lon.at[2 * a + i], r_lon.at[2 * a + i], {"lon": where})
            cp.start()
            lon_copies.append(cp)
    for cp in lon_copies:
        cp.wait()

    def get(ref, *k):
        return jnp.concatenate([ref[(*k, pl.ds(0, 8))], ref[(*k, pl.ds(total - 8, 8))]], axis=0)

    x_phase(fields, wet, mx, my, C, L, R, T, H, get, pl.ds(0, 16), 16, 4)
    for p in range(WIDE):
        Mn[4 * p : 4 * p + 4, :] = T[p, 12:16, :]
    for p in range(THIN):
        n = 4 * WIDE + 2 * p
        Mn[n : n + 2, :] = T[WIDE + p, 14:16, :]
    a_copies = []
    for d in range(1, LOW):
        cp = send(Mn, RA.at[low], s_a.at[d], r_a.at[d], {"lon": high * LOW + lax.rem(low + d, LOW)})
        cp.start()
        a_copies.append(cp)
    to_north = send(Mn, FS, s_lat.at[0], r_lat.at[0], {"lat": lat + 1})
    to_south = send(Ms, FN, s_lat.at[1], r_lat.at[1], {"lat": lat - 1})

    @pl.when(jnp.logical_not(last))
    def _():
        to_north.start()

    for p in range(WIDE):
        Ms[4 * p : 4 * p + 4, :] = T[p, 0:4, :]
    for p in range(THIN):
        n = 4 * WIDE + 2 * p
        Ms[n : n + 2, :] = T[WIDE + p, 0:2, :]

    @pl.when(jnp.logical_not(first))
    def _():
        to_south.start()

    RA[low] = Mn[...]
    for a in range(3):
        c_out[a] = C[a]
        l_out[a] = L[a]
        r_out[a] = R[a]
    for cp in a_copies:
        cp.wait()
    RB[high] = RA[lax.rem(tile[0], LOW)]
    b_copies = []
    for d in range(1, layers):
        cp = send(RB.at[high], RB.at[high], s_b.at[d], r_b.at[d], {"lon": lax.rem(high + d, layers) * LOW + low})
        cp.start()
        b_copies.append(cp)

    @pl.when(jnp.logical_not(last))
    def _():
        to_north.wait_send()
        to_south.wait_recv()
        north[...] = FN[...]

    @pl.when(jnp.logical_not(first))
    def _():
        to_south.wait_send()
        to_north.wait_recv()
        south[...] = FS[...]

    @pl.when(first)
    def _():
        south[...] = jnp.zeros((MSG, LANES), jnp.float32)

    for cp in b_copies:
        cp.wait()

    @pl.when(last)
    def _():
        x = RB[tile[0] // LOW]
        lane = lane_of(MSG)
        row = lax.broadcasted_iota(jnp.int32, (MSG, LANES), 0)
        flip = jnp.take_along_axis(x, LANES - 1 - lane, axis=1)
        swap = jnp.where(lane % 8 == 0, roll(x, 1), roll(x, -1))
        w = 4 * WIDE
        packed = (
            ((row >= 4 * SP) & (row < w))
            | ((row >= w + 2 * (VMP - WIDE)) & (row < w + 2 * (WET - WIDE)))
            | ((row >= w + 2 * (WETP - WIDE)) & (row < w + 2 * (MY - WIDE)))
            | (row >= w + 2 * (MYP - WIDE))
        )
        minus = (
            ((row >= 64) & (row < 4 * SP))
            | ((row >= 4 * SP + 4) & (row < w))
            | ((row >= w) & (row < w + 2 * (WET - WIDE)))
        )
        y = jnp.where(packed, swap, flip)
        back[...] = jnp.where(minus, -y, y)
        for p in range(WIDE):
            for i in range(4):
                north[4 * p + i : 4 * p + i + 1, :] = back[4 * p + 3 - i : 4 * p + 4 - i, :]
        for p in range(THIN):
            n = w + 2 * p
            for i in range(2):
                north[n + i : n + i + 1, :] = back[n + 1 - i : n + 2 - i, :]


BASE = 16


def step_kernel(
    coef, t, s, u, v, wet, mx, my, c, l, r, south, north, idf, o0, o1, o2, o3, T, H, E, F, A, WY, U, INV, FAC
):
    total = t.shape[1]

    def get(ref, *k):
        return ref[k] if k else ref[...]

    x_phase((t, s, u, v), wet, mx, my, c, l, r, T, H, get, pl.ds(BASE, total), total, 1)
    factorize(T, idf, U, INV, FAC, BASE, total)
    top = BASE + total
    for p in range(WIDE):
        T[p, BASE - 4 : BASE, :] = south[4 * p : 4 * p + 4, :]
        T[p, top : top + 4, :] = north[4 * p : 4 * p + 4, :]
    for p in range(THIN):
        n = 4 * WIDE + 2 * p
        T[WIDE + p, BASE - 2 : BASE, :] = south[n : n + 2, :]
        T[WIDE + p, top : top + 2, :] = north[n : n + 2, :]
    y_phase(T, E, F, A, WY, tuple((BASE - 8 + i, 48) for i in range(0, total + 16, 48)))

    def tile(i, carry):
        a = pl.multiple_of(i * 16, 16)
        finish(T, A, WY, U, INV, FAC, coef, (o0, o1, o2, o3), a + BASE, a, 16)
        return carry

    lax.fori_loop(0, total // 16, tile, 0)


def vspec():
    return pl.BlockSpec(memory_space=pltpu.VMEM)


def sspec():
    return pl.BlockSpec(memory_space=pltpu.SMEM)


def shards(heat, salt, east, north, water, mx, my, idf, spreading, mirror):
    f32 = jnp.float32
    total = heat.shape[1]
    lon_n, lat_n = lax.axis_size("lon"), lax.axis_size("lat")
    layers = lon_n // LOW
    fields = (heat, salt, east, north)
    tile = mirror[:1] // LANES
    stack = jax.ShapeDtypeStruct((3, total, LANES), f32)
    msg = jax.ShapeDtypeStruct((MSG, LANES), f32)

    def vm(*shape):
        return pltpu.VMEM((*shape, LANES), f32)

    def dma(n):
        return pltpu.SemaphoreType.DMA((n,))

    halos = pl.pallas_call(
        functools.partial(halo_kernel, lon_n, lat_n),
        out_shape=[stack] * 3 + [msg] * 2,
        in_specs=[sspec()] + [vspec()] * 7,
        out_specs=[vspec()] * 5,
        scratch_shapes=[vm(3, total)] * 3
        + [vm(PLANES, 16), vm(7, 16)]
        + [vm(MSG)] * 4
        + [vm(LOW, MSG), vm(layers, MSG), vm(MSG)]
        + [dma(6), dma(6), dma(2), dma(2), dma(LOW), dma(LOW), dma(layers), dma(layers)],
        compiler_params=pltpu.CompilerParams(
            collective_id=0, has_side_effects=True, vmem_limit_bytes=VMEM_LIMIT
        ),
    )(tile, *fields, water, mx, my)

    tall = total + 2 * BASE
    out = jax.ShapeDtypeStruct((8, total, LANES), f32)
    outs = pl.pallas_call(
        step_kernel,
        out_shape=[out] * 4,
        in_specs=[sspec()] + [vspec()] * 13,
        out_specs=[vspec()] * 4,
        scratch_shapes=[vm(PLANES, tall), vm(7, total), vm(4, tall), vm(4, tall), vm(WIDE, tall), vm(8, tall)]
        + [vm(7, total), vm(8, total), vm(7, total)],
        compiler_params=pltpu.CompilerParams(vmem_limit_bytes=VMEM_LIMIT),
    )(spreading, *fields, water, mx, my, *halos, idf)
    return tuple(outs)


def solution(mesh):
    deep = P(None, "lat", "lon")
    flat = P("lat", "lon")
    return jax.shard_map(
        shards,
        mesh=mesh,
        in_specs=(deep,) * 5 + (flat, flat, deep, P(), P("lon")),
        out_specs=(deep,) * 4,
        check_vma=False,
    )
```

profile of v0, /device:TPU:1, one launch (start us, length us, event | category | flops | bytes accessed | tf_op | source)
XLA Modules:
  0.0 55.8 jit_solution(14914779622439257117)
XLA Ops:
  0.6 0.0 copy-start
  0.6 0.6 %copy-done = s32[128]{0:T(128)S(1)} copy-done((s32[128]{0:T(128)S(1)}, s32[128]{0:T(128)}, u32[]{:S(2)}) %copy-start) | copy-done | bytes 536
  1.4 28.2 %shard_map.129 = (f32[3,128,128]{2,1,0:T(8,128)}, f32[3,128,128]{2,1,0:T(8,128)}, f32[3,128,128]{2,1,0:T(8,128)}, f32[176,128]{1,0:T(8,128)}, f32[176,128]{1,0:T(8,128)}) custom-call(s32[1]{0:T(128)S(6)} %select_n.5.tile, f32[8,128,128]{2,1,0:T(8,128)} %t.3, f32[8,128,128]{2,1,0:T(8,128)} %s.3, f32[8,128,128]{2,1,0:T(8,128)} %u.3, f32[8,128,128]{2,1,0:T(8,128)} %v.3, ...), custom_call_target="tpu_custom_call" | custom-call | tf_op jit(solution)/shard_map/pallas_call | solution.py:466
  29.6 26.2 %shard_map.130 = (f32[8,128,128]{2,1,0:T(8,128)}, f32[8,128,128]{2,1,0:T(8,128)}, f32[8,128,128]{2,1,0:T(8,128)}, f32[8,128,128]{2,1,0:T(8,128)}) custom-call(f32[4,8]{1,0:T(4,128)} %coef.1, f32[8,128,128]{2,1,0:T(8,128)} %t.3, f32[8,128,128]{2,1,0:T(8,128)} %s.3, f32[8,128,128]{2,1,0:T(8,128)} %u.3, f32[8,128,128]{2,1,0:T(8,128)} %v.3, s32[8,128,128]{2,1,0:T(8,128)} %wet.3, ...), custom_call_target="tpu_custom_call" | custom-call | tf_op jit(solution)/shard_map/pallas_call | solution.py:483
Async XLA Ops:
  0.6 0.7 %copy-start = (s32[128]{0:T(128)S(1)}, s32[128]{0:T(128)}, u32[]{:S(2)}) copy-start(s32[128]{0:T(128)} %param.19) | copy-start | bytes 1540
where the time goes:
time: 56.3 us; the launch traced here: 55.8 us
  Pallas kernels  54.3 us (96%)
  between operations  0.81 us (1%)
  local copies, waits for them, and re-layouts  0.65 us (1%)
    pallas_call x1, Pallas kernels, shards(): pl.pallas_call(functools.partial(halo_kernel, lon_n, lat_n), out_shape=[s...  28.2 us
    pallas_call x1, Pallas kernels, shards(): pl.pallas_call(step_kernel, out_shape=[out] * 4, in_specs=[sspec()] + [vs...  26.2 us

commit v1 on v0

--- a/solution.py
+++ b/solution.py
@@ -126,51 +126,63 @@
     return lf, [jnp.where(low, re[a], le[a]) for a in range(2)]
 
 
-def x_phase(fields, wet_ref, mx_ref, my_ref, c_ref, l_ref, r_ref, T, H, get, tr, rows, unroll):
-    lane = lane_of(rows)
+CHUNK = 16
+
+
+def x_prepare(mx_ref, my_ref, c_ref, l_ref, r_ref, T, H, get, base, count):
+    lane = lane_of(CHUNK)
     low = lane % 8 < 4
-    lf, le = packed_x(c_ref, l_ref, r_ref, T, get, tr, rows)
-    for a in range(3):
-        H[a] = jnp.where(low, get(r_ref, a), get(l_ref, a))
-    for a in range(2):
-        H[3 + a] = lf[a]
-        H[5 + a] = le[a]
-    mx = get(mx_ref)
-    my = get(my_ref)
-    T[MY, tr, :] = my
-    mxh = group_roll(H[2], 8)
-    mx1 = shifted(mx, mxh, 1, lane)
-
-    def level(k, carry):
-        wet = get(wet_ref, k).astype(jnp.float32)
+    for c in range(count):
+        tr, hr = pl.ds(base + CHUNK * c, CHUNK), pl.ds(CHUNK * c, CHUNK)
+        lf, le = packed_x(c_ref, l_ref, r_ref, T, functools.partial(get, c), tr, CHUNK)
+        for a in range(3):
+            h = jnp.where(low, get(c, r_ref, a), get(c, l_ref, a))
+            H[a, hr, :] = h
+        for a in range(2):
+            H[3 + a, hr, :] = lf[a]
+            H[5 + a, hr, :] = le[a]
+        T[MY, tr, :] = get(c, my_ref)
+        mxh = group_roll(h, 8)
+        H[7, hr, :] = mxh
+        H[8, hr, :] = shifted(get(c, mx_ref), mxh, 1, lane)
+
+
+def x_levels(fields, wet_ref, mx_ref, my_ref, T, H, get, base, count, first, end, unroll):
+    lane = lane_of(CHUNK)
+
+    def part(k, c):
+        tr, hr = pl.ds(base + CHUNK * c, CHUNK), pl.ds(CHUNK * c, CHUNK)
+        mx, mxh, mx1 = get(c, mx_ref), H[7, hr, :], H[8, hr, :]
+        wet = get(c, wet_ref, k).astype(jnp.float32)
         T[WET + k, tr, :] = wet
-        hwet = group_roll(H[2], k)
+        hwet = group_roll(H[2, hr, :], k)
         opening = wet * shifted(wet, hwet, 1, lane)
         T[WX + k, tr, :] = 0.5 * (mx + mx1) * opening
-        hu = group_roll(H[1], k)
-        um = get(fields[2], k) * wet * mx
+        hu = group_roll(H[1, hr, :], k)
+        um = get(c, fields[2], k) * wet * mx
         cf = coefs(0.5 * (um + shifted(um, hu * mxh, 1, lane)), opening)
         for f in range(4):
-            q = get(fields[f], k) * wet
+            q = get(c, fields[f], k) * wet
             if f == 3:
-                T[VM + k, tr, :] = q * my
+                T[VM + k, tr, :] = q * get(c, my_ref)
             g = 8 * (f % 2) + k
-            h = hu if f == 2 else group_roll(H[f // 2], g)
+            h = hu if f == 2 else group_roll(H[f // 2, hr, :], g)
             qm, q1, q2 = (shifted(q, h, s, lane) for s in (-1, 1, 2))
             ed = edge(qm, q, q1, q2)
-            he = group_roll(H[5 + f // 2], g)
+            he = group_roll(H[5 + f // 2, hr, :], g)
             em = roll(jnp.where(lane == LANES - 1, he, ed), 1)
             e1 = roll(jnp.where(lane == 0, he, ed), -1)
             fl = flux(cf, em, ed, e1, q, q1)
-            flm = roll(jnp.where(lane == LANES - 1, group_roll(H[3 + f // 2], g), fl), 1)
+            flm = roll(jnp.where(lane == LANES - 1, group_roll(H[3 + f // 2, hr, :], g), fl), 1)
             T[8 * f + k, tr, :] = q + flm - fl
 
     def levels(i, carry):
         for j in range(unroll):
-            level(i * unroll + j, 0)
+            for c in range(count):
+                part(i * unroll + j, c)
         return carry
 
-    lax.fori_loop(0, 8 // unroll, levels, 0)
+    lax.fori_loop(first // unroll, end // unroll, levels, 0)
 
 
 def face_y(T, vm, wet, my, WY, kw, r0, rows):
@@ -268,9 +280,12 @@
 MESH = pl.DeviceIdType.MESH
 
 
-def halo_kernel(
-    lon_n, lat_n, tile, t, s, u, v, wet, mx, my, c_out, l_out, r_out, south, north,
-    C, L, R, T, H, Mn, Ms, FS, FN, RA, RB, back,
+BASE = 16
+
+
+def step_kernel(
+    lon_n, lat_n, tile, coef, t, s, u, v, wet, mx, my, idf, o0, o1, o2, o3,
+    C, L, R, TE, HE, Mn, Ms, FS, FN, RA, RB, back, T, H, E, F, A, WY, U, INV, FAC,
     s_lon, r_lon, s_lat, r_lat, s_a, r_a, s_b, r_b,
 ):
     total = t.shape[1]
@@ -314,15 +329,19 @@
     for cp in lon_copies:
         cp.wait()
 
-    def get(ref, *k):
+    def ends(c, ref, *k):
         return jnp.concatenate([ref[(*k, pl.ds(0, 8))], ref[(*k, pl.ds(total - 8, 8))]], axis=0)
 
-    x_phase(fields, wet, mx, my, C, L, R, T, H, get, pl.ds(0, 16), 16, 4)
+    def get(c, ref, *k):
+        return ref[(*k, pl.ds(CHUNK * c, CHUNK))]
+
+    x_prepare(mx, my, C, L, R, TE, HE, ends, 0, 1)
+    x_levels(fields, wet, mx, my, TE, HE, ends, 0, 1, 0, 8, 4)
     for p in range(WIDE):
-        Mn[4 * p : 4 * p + 4, :] = T[p, 12:16, :]
+        Mn[4 * p : 4 * p + 4, :] = TE[p, 12:16, :]
     for p in range(THIN):
         n = 4 * WIDE + 2 * p
-        Mn[n : n + 2, :] = T[WIDE + p, 14:16, :]
+        Mn[n : n + 2, :] = TE[WIDE + p, 14:16, :]
     a_copies = []
     for d in range(1, LOW):
         cp = send(Mn, RA.at[low], s_a.at[d], r_a.at[d], {"lon": high * LOW + lax.rem(low + d, LOW)})
@@ -336,20 +355,19 @@
         to_north.start()
 
     for p in range(WIDE):
-        Ms[4 * p : 4 * p + 4, :] = T[p, 0:4, :]
+        Ms[4 * p : 4 * p + 4, :] = TE[p, 0:4, :]
     for p in range(THIN):
         n = 4 * WIDE + 2 * p
-        Ms[n : n + 2, :] = T[WIDE + p, 0:2, :]
+        Ms[n : n + 2, :] = TE[WIDE + p, 0:2, :]
 
     @pl.when(jnp.logical_not(first))
     def _():
         to_south.start()
 
     RA[low] = Mn[...]
-    for a in range(3):
-        c_out[a] = C[a]
-        l_out[a] = L[a]
-        r_out[a] = R[a]
+    count = total // CHUNK
+    x_prepare(mx, my, C, L, R, T, H, get, BASE, count)
+    x_levels(fields, wet, mx, my, T, H, get, BASE, count, 0, 2, 1)
     for cp in a_copies:
         cp.wait()
     RB[high] = RA[lax.rem(tile[0], LOW)]
@@ -359,21 +377,33 @@
         cp.start()
         b_copies.append(cp)
 
+    x_levels(fields, wet, mx, my, T, H, get, BASE, count, 2, 8, 1)
+    factorize(T, idf, U, INV, FAC, BASE, total)
+
+    def spread(src, wide, thin):
+        for p in range(WIDE):
+            T[p, wide : wide + 4, :] = src[4 * p : 4 * p + 4, :]
+        for p in range(THIN):
+            n = 4 * WIDE + 2 * p
+            T[WIDE + p, thin : thin + 2, :] = src[n : n + 2, :]
+
+    top = BASE + total
+
     @pl.when(jnp.logical_not(last))
     def _():
         to_north.wait_send()
         to_south.wait_recv()
-        north[...] = FN[...]
+        spread(FN, top, top)
 
     @pl.when(jnp.logical_not(first))
     def _():
         to_south.wait_send()
         to_north.wait_recv()
-        south[...] = FS[...]
+        spread(FS, BASE - 4, BASE - 2)
 
     @pl.when(first)
     def _():
-        south[...] = jnp.zeros((MSG, LANES), jnp.float32)
+        T[:, BASE - 8 : BASE, :] = jnp.zeros((PLANES, 8, LANES), jnp.float32)
 
     for cp in b_copies:
         cp.wait()
@@ -401,42 +431,20 @@
         back[...] = jnp.where(minus, -y, y)
         for p in range(WIDE):
             for i in range(4):
-                north[4 * p + i : 4 * p + i + 1, :] = back[4 * p + 3 - i : 4 * p + 4 - i, :]
+                T[p, top + i : top + i + 1, :] = back[4 * p + 3 - i : 4 * p + 4 - i, :]
         for p in range(THIN):
             n = w + 2 * p
             for i in range(2):
-                north[n + i : n + i + 1, :] = back[n + 1 - i : n + 2 - i, :]
-
-
-BASE = 16
-
-
-def step_kernel(
-    coef, t, s, u, v, wet, mx, my, c, l, r, south, north, idf, o0, o1, o2, o3, T, H, E, F, A, WY, U, INV, FAC
-):
-    total = t.shape[1]
-
-    def get(ref, *k):
-        return ref[k] if k else ref[...]
-
-    x_phase((t, s, u, v), wet, mx, my, c, l, r, T, H, get, pl.ds(BASE, total), total, 1)
-    factorize(T, idf, U, INV, FAC, BASE, total)
-    top = BASE + total
-    for p in range(WIDE):
-        T[p, BASE - 4 : BASE, :] = south[4 * p : 4 * p + 4, :]
-        T[p, top : top + 4, :] = north[4 * p : 4 * p + 4, :]
-    for p in range(THIN):
-        n = 4 * WIDE + 2 * p
-        T[WIDE + p, BASE - 2 : BASE, :] = south[n : n + 2, :]
-        T[WIDE + p, top : top + 2, :] = north[n : n + 2, :]
-    y_phase(T, E, F, A, WY, tuple((BASE - 8 + i, 48) for i in range(0, total + 16, 48)))
-
-    def tile(i, carry):
+                T[WIDE + p, top + i : top + i + 1, :] = back[n + 1 - i : n + 2 - i, :]
+
+    y_phase(T, E, F, A, WY, tuple((BASE - 8 + i, 24) for i in range(0, total + 16, 24)))
+
+    def tile_rows(i, carry):
         a = pl.multiple_of(i * 16, 16)
         finish(T, A, WY, U, INV, FAC, coef, (o0, o1, o2, o3), a + BASE, a, 16)
         return carry
 
-    lax.fori_loop(0, total // 16, tile, 0)
+    lax.fori_loop(0, total // 16, tile_rows, 0)
 
 
 def vspec():
@@ -448,47 +456,36 @@
 
 
 def shards(heat, salt, east, north, water, mx, my, idf, spreading, mirror):
-    f32 = jnp.float32
     total = heat.shape[1]
     lon_n, lat_n = lax.axis_size("lon"), lax.axis_size("lat")
     layers = lon_n // LOW
     fields = (heat, salt, east, north)
     tile = mirror[:1] // LANES
-    stack = jax.ShapeDtypeStruct((3, total, LANES), f32)
-    msg = jax.ShapeDtypeStruct((MSG, LANES), f32)
+    tall = total + 2 * BASE
+    out = jax.ShapeDtypeStruct((8, total, LANES), jnp.float32)
 
     def vm(*shape):
-        return pltpu.VMEM((*shape, LANES), f32)
+        return pltpu.VMEM((*shape, LANES), jnp.float32)
 
     def dma(n):
         return pltpu.SemaphoreType.DMA((n,))
 
-    halos = pl.pallas_call(
-        functools.partial(halo_kernel, lon_n, lat_n),
-        out_shape=[stack] * 3 + [msg] * 2,
-        in_specs=[sspec()] + [vspec()] * 7,
-        out_specs=[vspec()] * 5,
+    outs = pl.pallas_call(
+        functools.partial(step_kernel, lon_n, lat_n),
+        out_shape=[out] * 4,
+        in_specs=[sspec(), sspec()] + [vspec()] * 8,
+        out_specs=[vspec()] * 4,
         scratch_shapes=[vm(3, total)] * 3
-        + [vm(PLANES, 16), vm(7, 16)]
+        + [vm(PLANES, 16), vm(9, 16)]
         + [vm(MSG)] * 4
         + [vm(LOW, MSG), vm(layers, MSG), vm(MSG)]
+        + [vm(PLANES, tall), vm(9, total), vm(4, tall), vm(4, tall), vm(WIDE, tall), vm(8, tall)]
+        + [vm(7, total), vm(8, total), vm(7, total)]
         + [dma(6), dma(6), dma(2), dma(2), dma(LOW), dma(LOW), dma(layers), dma(layers)],
         compiler_params=pltpu.CompilerParams(
             collective_id=0, has_side_effects=True, vmem_limit_bytes=VMEM_LIMIT
         ),
-    )(tile, *fields, water, mx, my)
-
-    tall = total + 2 * BASE
-    out = jax.ShapeDtypeStruct((8, total, LANES), f32)
-    outs = pl.pallas_call(
-        step_kernel,
-        out_shape=[out] * 4,
-        in_specs=[sspec()] + [vspec()] * 13,
-        out_specs=[vspec()] * 4,
-        scratch_shapes=[vm(PLANES, tall), vm(7, total), vm(4, tall), vm(4, tall), vm(WIDE, tall), vm(8, tall)]
-        + [vm(7, total), vm(8, total), vm(7, total)],
-        compiler_params=pltpu.CompilerParams(vmem_limit_bytes=VMEM_LIMIT),
-    )(spreading, *fields, water, mx, my, *halos, idf)
+    )(tile, spreading, *fields, water, mx, my, idf)
     return tuple(outs)
 
 

time: 56.3 us -> 80.2 us (1.42)
  Pallas kernels: 54.3 us -> 73.3 us
  local copies, waits for them, and re-layouts: 0.65 us -> 5.83 us
    pallas_call x2 -> x1, Pallas kernels: 54.3 us -> 73.3 us  [shards(): pl.pallas_call(functools.partial(step_kernel, lon_n, lat_n), out_shape=[o...]
    unnamed x2 -> x12, local copies, waits for them, and re-layouts: 0.65 us -> 5.83 us
where the time goes in v1:
time: 80.2 us; the launch traced here: 79.9 us
  Pallas kernels  73.3 us (91%)
  local copies, waits for them, and re-layouts  5.83 us (7%)
  between operations  0.82 us (1%)
    pallas_call x1, Pallas kernels, shards(): pl.pallas_call(functools.partial(step_kernel, lon_n, lat_n), out_shape=[o...  73.3 us
    unnamed x12, local copies, waits for them, and re-layouts  5.83 us

profile of v1, /device:TPU:1, one launch (start us, length us, event | category | flops | bytes accessed | tf_op | source)
XLA Modules:
  0.0 79.9 jit_solution(12311602579656536595)
XLA Ops:
  0.6 0.0 copy-start.3
  0.6 0.6 copy-done.3
  1.5 73.3 %shard_map.129 = (f32[8,128,128]{2,1,0:T(8,128)}, f32[8,128,128]{2,1,0:T(8,128)}, f32[8,128,128]{2,1,0:T(8,128)}, f32[8,128,128]{2,1,0:T(8,128)}) custom-call(s32[1]{0:T(128)S(6)} %select_n.5.tile, f32[4,8]{1,0:T(4,128)} %coef.1, f32[8,128,128]{2,1,0:T(8,128)} %t.1, f32[8,128,128]{2,1,0:T(8,128)} %s.1, f32[8,128,128]{2,1,0:T(8,128)} %u.1, f32[8,128,128]{2,1,0:T(8,128)} %v.1, ...), custom_call_target="tpu_custom_call" | custom-call | tf_op jit(solution)/shard_map/pallas_call | solution.py:473
  74.8 0.0 copy-start.2
  74.8 1.9 %copy.18 = f32[8,128,128]{2,1,0:T(8,128)} copy(f32[8,128,128]{2,1,0:T(8,128)} %get-tuple-element.8) | data formatting | bytes 1048576
  76.7 0.0 copy-done.2
  76.7 0.0 copy-start.1
  76.7 0.8 copy.19
  77.5 0.4 copy-done.1
  77.9 0.0 copy-start
  77.9 0.8 copy.20
  78.7 0.4 copy-done
  79.2 0.8 copy.21
Async XLA Ops:
  0.6 0.7 copy-start.3
  74.8 1.9 %copy-start.2 = (f32[8,128,128]{2,1,0:T(8,128)S(1)}, f32[8,128,128]{2,1,0:T(8,128)}, u32[]{:S(2)}) copy-start(f32[8,128,128]{2,1,0:T(8,128)} %get-tuple-element.9) | copy-start | bytes 1572868
  76.7 1.2 %copy-start.1 = (f32[8,128,128]{2,1,0:T(8,128)S(1)}, f32[8,128,128]{2,1,0:T(8,128)}, u32[]{:S(2)}) copy-start(f32[8,128,128]{2,1,0:T(8,128)} %get-tuple-element.10) | copy-start | bytes 1572868
  77.9 1.2 %copy-start = (f32[8,128,128]{2,1,0:T(8,128)S(1)}, f32[8,128,128]{2,1,0:T(8,128)}, u32[]{:S(2)}) copy-start(f32[8,128,128]{2,1,0:T(8,128)} %get-tuple-element.11) | copy-start | bytes 1572868

commit v2 on v1

--- a/solution.py
+++ b/solution.py
@@ -11,7 +11,7 @@
 SP, VM, VMP, WET, WETP, MY, MYP, WX, WXP, PLANES = 32, 34, 42, 43, 51, 52, 53, 54, 62, 63
 WIDE, THIN = 34, 20
 MSG = WIDE * 4 + THIN * 2
-VMEM_LIMIT = 56 * 1024 * 1024
+VMEM_LIMIT = 32 * 1024 * 1024
 
 
 def lane_of(rows):
@@ -126,10 +126,7 @@
     return lf, [jnp.where(low, re[a], le[a]) for a in range(2)]
 
 
-CHUNK = 16
-
-
-def x_prepare(mx_ref, my_ref, c_ref, l_ref, r_ref, T, H, get, base, count):
+def x_prepare(mx_ref, my_ref, c_ref, l_ref, r_ref, T, H, get, base, count, CHUNK):
     lane = lane_of(CHUNK)
     low = lane % 8 < 4
     for c in range(count):
@@ -147,24 +144,25 @@
         H[8, hr, :] = shifted(get(c, mx_ref), mxh, 1, lane)
 
 
-def x_levels(fields, wet_ref, mx_ref, my_ref, T, H, get, base, count, first, end, unroll):
+def x_levels(fields, wet_ref, mx_ref, my_ref, T, H, get, base, count, first, end, unroll, CHUNK):
     lane = lane_of(CHUNK)
 
     def part(k, c):
+        out = []
         tr, hr = pl.ds(base + CHUNK * c, CHUNK), pl.ds(CHUNK * c, CHUNK)
         mx, mxh, mx1 = get(c, mx_ref), H[7, hr, :], H[8, hr, :]
         wet = get(c, wet_ref, k).astype(jnp.float32)
-        T[WET + k, tr, :] = wet
+        out.append((WET + k, tr, wet))
         hwet = group_roll(H[2, hr, :], k)
         opening = wet * shifted(wet, hwet, 1, lane)
-        T[WX + k, tr, :] = 0.5 * (mx + mx1) * opening
+        out.append((WX + k, tr, 0.5 * (mx + mx1) * opening))
         hu = group_roll(H[1, hr, :], k)
         um = get(c, fields[2], k) * wet * mx
         cf = coefs(0.5 * (um + shifted(um, hu * mxh, 1, lane)), opening)
         for f in range(4):
             q = get(c, fields[f], k) * wet
             if f == 3:
-                T[VM + k, tr, :] = q * get(c, my_ref)
+                out.append((VM + k, tr, q * get(c, my_ref)))
             g = 8 * (f % 2) + k
             h = hu if f == 2 else group_roll(H[f // 2, hr, :], g)
             qm, q1, q2 = (shifted(q, h, s, lane) for s in (-1, 1, 2))
@@ -174,46 +172,47 @@
             e1 = roll(jnp.where(lane == 0, he, ed), -1)
             fl = flux(cf, em, ed, e1, q, q1)
             flm = roll(jnp.where(lane == LANES - 1, group_roll(H[3 + f // 2, hr, :], g), fl), 1)
-            T[8 * f + k, tr, :] = q + flm - fl
+            out.append((8 * f + k, tr, q + flm - fl))
+
+        return out
 
     def levels(i, carry):
-        for j in range(unroll):
-            for c in range(count):
-                part(i * unroll + j, c)
+        for c in range(count):
+            stores = []
+            for j in range(unroll):
+                stores += part(i * unroll + j, c)
+            for p, tr, x in stores:
+                T[p, tr, :] = x
         return carry
 
     lax.fori_loop(first // unroll, end // unroll, levels, 0)
 
 
-def face_y(T, vm, wet, my, WY, kw, r0, rows):
-    r, r1 = pl.ds(r0, rows), pl.ds(r0 + 1, rows)
-    opening = T[wet, r, :] * T[wet, r1, :]
+def y_advect(T, A, WY, planes, vm, wet, my, kw, r0, rows):
+    f0, fr = r0 - 8, rows + 8
+    at = pl.ds(f0, fr)
+    a1 = pl.ds(f0 + 1, fr)
+    opening = T[wet, at, :] * T[wet, a1, :]
+    cf = coefs(0.5 * (T[vm, at, :] + T[vm, a1, :]), opening)
+    stores = []
     if WY is not None:
-        WY[kw, r, :] = 0.5 * (T[my, r, :] + T[my, r1, :]) * opening
-    return coefs(0.5 * (T[vm, r, :] + T[vm, r1, :]), opening)
-
-
-def y_advect(T, E, F, A, WY, planes, vm, wet, my, kw, chunks):
+        stores.append((WY, kw, at, 0.5 * (T[my, at, :] + T[my, a1, :]) * opening))
+    for p in planes:
+        q = [T[p, pl.ds(f0 + s, fr), :] for s in (-2, -1, 0, 1, 2, 3)]
+        em, e0, e1 = (edge(*q[i : i + 4]) for i in range(3))
+        fl = flux(cf, em, e0, e1, q[2], q[3])
+        stores.append((A, p, pl.ds(r0, rows), q[2][8:] + fl[7 : 7 + rows] - fl[8:]))
+    for ref, p, r, x in stores:
+        ref[p, r, :] = x
+
+
+def y_phase(T, A, WY, chunks):
     for r0, rows in chunks:
-        for n, p in enumerate(planes):
-            E[n, pl.ds(r0, rows), :] = edge(*(T[p, pl.ds(r0 + s, rows), :] for s in (-1, 0, 1, 2)))
-    for r0, rows in chunks:
-        cf = face_y(T, vm, wet, my, WY, kw, r0, rows)
-        for n, p in enumerate(planes):
-            em, e0, e1 = (E[n, pl.ds(r0 + s, rows), :] for s in (-1, 0, 1))
-            q0, q1 = (T[p, pl.ds(r0 + s, rows), :] for s in (0, 1))
-            F[n, pl.ds(r0, rows), :] = flux(cf, em, e0, e1, q0, q1)
-    for r0, rows in chunks:
-        for n, p in enumerate(planes):
-            r = pl.ds(r0, rows)
-            A[p, r, :] = T[p, r, :] + F[n, pl.ds(r0 - 1, rows), :] - F[n, r, :]
-
-
-def y_phase(T, E, F, A, WY, chunks):
-    y_advect(T, E, F, A, None, (SP, SP + 1), VMP, WETP, MYP, 0, chunks)
+        y_advect(T, A, None, (SP, SP + 1), VMP, WETP, MYP, 0, r0, rows)
 
     def level(k, carry):
-        y_advect(T, E, F, A, WY, tuple(8 * f + k for f in range(4)), VM + k, WET + k, MY, k, chunks)
+        for r0, rows in chunks:
+            y_advect(T, A, WY, tuple(8 * f + k for f in range(4)), VM + k, WET + k, MY, k, r0, rows)
         return carry
 
     lax.fori_loop(0, 8, level, 0)
@@ -248,6 +247,8 @@
     wxp = T[WXP, r, :]
     ap = [A[SP + a, r, :] for a in range(2)]
     reduced = []
+    wets = [T[WET + k, r, :] for k in range(8)]
+    facs = [FAC[k, o, :] for k in range(7)]
     for k in range(8):
         wx = T[WX + k, r, :]
         wxm = roll(jnp.where(lane == LANES - 1, roll(wxp, -8 * k), wx), 1)
@@ -266,26 +267,24 @@
                 d = d + U[k - 1, o, :] * reduced[-1][f]
             row.append(d * inv)
         reduced.append(row)
-    x = reduced[7]
-    for k in range(7, -1, -1):
-        if k < 7:
-            factor = FAC[k, o, :]
-            x = [reduced[k][f] + factor * x[f] for f in range(4)]
-        wet = T[WET + k, r, :]
+    solved = [reduced[7]]
+    for k in range(6, -1, -1):
+        solved.insert(0, [reduced[k][f] + facs[k] * solved[0][f] for f in range(4)])
+    for k in range(8):
         for f in range(4):
-            outs[f][k, o, :] = x[f] * wet
+            outs[f][k, o, :] = solved[k][f] * wets[k]
 
 
 LOW = 4
 MESH = pl.DeviceIdType.MESH
 
 
-BASE = 16
-
-
-def step_kernel(
-    lon_n, lat_n, tile, coef, t, s, u, v, wet, mx, my, idf, o0, o1, o2, o3,
-    C, L, R, TE, HE, Mn, Ms, FS, FN, RA, RB, back, T, H, E, F, A, WY, U, INV, FAC,
+BASE = 24
+
+
+def zonal_kernel(
+    lon_n, lat_n, tile, t, s, u, v, wet, mx, my, T,
+    C, L, R, TE, HE, Mn, Ms, FS, FN, RA, RB, back, H,
     s_lon, r_lon, s_lat, r_lat, s_a, r_a, s_b, r_b,
 ):
     total = t.shape[1]
@@ -333,10 +332,10 @@
         return jnp.concatenate([ref[(*k, pl.ds(0, 8))], ref[(*k, pl.ds(total - 8, 8))]], axis=0)
 
     def get(c, ref, *k):
-        return ref[(*k, pl.ds(CHUNK * c, CHUNK))]
-
-    x_prepare(mx, my, C, L, R, TE, HE, ends, 0, 1)
-    x_levels(fields, wet, mx, my, TE, HE, ends, 0, 1, 0, 8, 4)
+        return ref[(*k, pl.ds(64 * c, 64))]
+
+    x_prepare(mx, my, C, L, R, TE, HE, ends, 0, 1, 16)
+    x_levels(fields, wet, mx, my, TE, HE, ends, 0, 1, 0, 8, 4, 16)
     for p in range(WIDE):
         Mn[4 * p : 4 * p + 4, :] = TE[p, 12:16, :]
     for p in range(THIN):
@@ -365,9 +364,9 @@
         to_south.start()
 
     RA[low] = Mn[...]
-    count = total // CHUNK
-    x_prepare(mx, my, C, L, R, T, H, get, BASE, count)
-    x_levels(fields, wet, mx, my, T, H, get, BASE, count, 0, 2, 1)
+    count = total // 64
+    x_prepare(mx, my, C, L, R, T, H, get, BASE, count, 64)
+    x_levels(fields, wet, mx, my, T, H, get, BASE, count, 0, 2, 1, 64)
     for cp in a_copies:
         cp.wait()
     RB[high] = RA[lax.rem(tile[0], LOW)]
@@ -377,8 +376,7 @@
         cp.start()
         b_copies.append(cp)
 
-    x_levels(fields, wet, mx, my, T, H, get, BASE, count, 2, 8, 1)
-    factorize(T, idf, U, INV, FAC, BASE, total)
+    x_levels(fields, wet, mx, my, T, H, get, BASE, count, 2, 8, 1, 64)
 
     def spread(src, wide, thin):
         for p in range(WIDE):
@@ -437,7 +435,11 @@
             for i in range(2):
                 T[WIDE + p, top + i : top + i + 1, :] = back[n + 1 - i : n + 2 - i, :]
 
-    y_phase(T, E, F, A, WY, tuple((BASE - 8 + i, 24) for i in range(0, total + 16, 24)))
+
+def meridional_kernel(coef, T, idf, o0, o1, o2, o3, A, WY, U, INV, FAC):
+    total = idf.shape[1]
+    factorize(T, idf, U, INV, FAC, BASE, total)
+    y_phase(T, A, WY, tuple((BASE - 8 + i, 48) for i in range(0, total + 16, 48)))
 
     def tile_rows(i, carry):
         a = pl.multiple_of(i * 16, 16)
@@ -470,22 +472,29 @@
     def dma(n):
         return pltpu.SemaphoreType.DMA((n,))
 
-    outs = pl.pallas_call(
-        functools.partial(step_kernel, lon_n, lat_n),
-        out_shape=[out] * 4,
-        in_specs=[sspec(), sspec()] + [vspec()] * 8,
-        out_specs=[vspec()] * 4,
+    stack = pl.pallas_call(
+        functools.partial(zonal_kernel, lon_n, lat_n),
+        out_shape=jax.ShapeDtypeStruct((PLANES, tall, LANES), jnp.float32),
+        in_specs=[sspec()] + [vspec()] * 7,
+        out_specs=vspec(),
         scratch_shapes=[vm(3, total)] * 3
         + [vm(PLANES, 16), vm(9, 16)]
         + [vm(MSG)] * 4
         + [vm(LOW, MSG), vm(layers, MSG), vm(MSG)]
-        + [vm(PLANES, tall), vm(9, total), vm(4, tall), vm(4, tall), vm(WIDE, tall), vm(8, tall)]
-        + [vm(7, total), vm(8, total), vm(7, total)]
+        + [vm(9, total)]
         + [dma(6), dma(6), dma(2), dma(2), dma(LOW), dma(LOW), dma(layers), dma(layers)],
         compiler_params=pltpu.CompilerParams(
             collective_id=0, has_side_effects=True, vmem_limit_bytes=VMEM_LIMIT
         ),
-    )(tile, spreading, *fields, water, mx, my, idf)
+    )(tile, *fields, water, mx, my)
+    outs = pl.pallas_call(
+        meridional_kernel,
+        out_shape=[out] * 4,
+        in_specs=[sspec()] + [vspec()] * 2,
+        out_specs=[vspec()] * 4,
+        scratch_shapes=[vm(WIDE, tall), vm(8, tall), vm(7, total), vm(8, total), vm(7, total)],
+        compiler_params=pltpu.CompilerParams(vmem_limit_bytes=VMEM_LIMIT),
+    )(spreading, stack, idf)
     return tuple(outs)
 
 

time: 80.2 us -> 55.2 us (0.69)
  Pallas kernels: 73.3 us -> 44.5 us
  between operations: 0.82 us -> 3.29 us
  local copies, waits for them, and re-layouts: 5.83 us -> 6.88 us
    pallas_call x1 -> x2, Pallas kernels: 73.3 us -> 44.5 us  [the longest x1 31.3 us: shards(): pl.pallas_call(functools.partial(zonal_kernel, lon_n, lat_n), out_shape=j...]
    unnamed x12 -> x18, local copies, waits for them, and re-layouts: 5.83 us -> 6.88 us
where the time goes in v2:
time: 55.2 us; the launch traced here: 54.7 us
  Pallas kernels  44.5 us (81%)
  local copies, waits for them, and re-layouts  6.88 us (12%)
  between operations  3.29 us (6%)
    pallas_call x1, Pallas kernels, shards(): pl.pallas_call(functools.partial(zonal_kernel, lon_n, lat_n), out_shape=j...  31.3 us
    pallas_call x1, Pallas kernels, shards(): pl.pallas_call(meridional_kernel, out_shape=[out] * 4, in_specs=[sspec()]...  13.2 us
    unnamed x18, local copies, waits for them, and re-layouts  6.88 us

profile of v2, /device:TPU:1, one launch (start us, length us, event | category | flops | bytes accessed | tf_op | source)
XLA Modules:
  0.0 54.7 jit_solution(10171962698479393192)
XLA Ops:
  0.6 0.0 copy-start.8
  3.3 0.0 copy-start
  3.3 1.0 %copy-done = f32[8,128,128]{2,1,0:T(8,128)S(1)} copy-done((f32[8,128,128]{2,1,0:T(8,128)S(1)}, f32[8,128,128]{2,1,0:T(8,128)}, u32[]{:S(2)}) %copy-start) | copy-done | bytes 524312
  4.3 0.0 copy-start.1
  4.3 1.0 %copy-done.1 = f32[8,128,128]{2,1,0:T(8,128)S(1)} copy-done((f32[8,128,128]{2,1,0:T(8,128)S(1)}, f32[8,128,128]{2,1,0:T(8,128)}, u32[]{:S(2)}) %copy-start.1) | copy-done | bytes 524312
  5.3 0.0 copy-start.2
  5.3 1.0 %copy-done.2 = f32[8,128,128]{2,1,0:T(8,128)S(1)} copy-done((f32[8,128,128]{2,1,0:T(8,128)S(1)}, f32[8,128,128]{2,1,0:T(8,128)}, u32[]{:S(2)}) %copy-start.2) | copy-done | bytes 524312
  6.4 0.0 copy-start.3
  6.4 1.0 %copy-done.3 = f32[8,128,128]{2,1,0:T(8,128)S(1)} copy-done((f32[8,128,128]{2,1,0:T(8,128)S(1)}, f32[8,128,128]{2,1,0:T(8,128)}, u32[]{:S(2)}) %copy-start.3) | copy-done | bytes 524312
  7.4 0.0 copy-start.4
  7.4 1.0 %copy-done.4 = s32[8,128,128]{2,1,0:T(8,128)S(1)} copy-done((s32[8,128,128]{2,1,0:T(8,128)S(1)}, s32[8,128,128]{2,1,0:T(8,128)}, u32[]{:S(2)}) %copy-start.4) | copy-done | bytes 524312
  8.5 0.0 copy-start.6
  8.5 0.8 %copy-done.6 = f32[128,128]{1,0:T(8,128)S(1)} copy-done((f32[128,128]{1,0:T(8,128)S(1)}, f32[128,128]{1,0:T(8,128)}, u32[]{:S(2)}) %copy-start.6) | copy-done | bytes 65560
  9.3 0.0 copy-start.7
  9.3 0.8 %copy-done.7 = f32[128,128]{1,0:T(8,128)S(1)} copy-done((f32[128,128]{1,0:T(8,128)S(1)}, f32[128,128]{1,0:T(8,128)}, u32[]{:S(2)}) %copy-start.7) | copy-done | bytes 65560
  10.1 0.0 copy-start.5
  10.2 31.3 %shard_map.129.T = f32[63,176,128]{2,1,0:T(8,128)S(1)} custom-call(s32[1]{0:T(128)S(6)} %select_n.5.tile, f32[8,128,128]{2,1,0:T(8,128)S(1)} %copy-done, f32[8,128,128]{2,1,0:T(8,128)S(1)} %copy-done.1, f32[8,128,128]{2,1,0:T(8,128)S(1)} %copy-done.2, f32[8,128,128]{2,1,0:T(8,128)S(1)} %copy-done.3, s32[8,128,128]{2,1,0:T(8,128)S(1)} %copy-done.4, ...), custom_call_target="tpu_custom_call" | custom-call | tf_op jit(solution)/shard_map/pallas_call | solution.py:475
  41.4 0.0 copy-done.8
  41.4 0.0 copy-done.5
  41.5 13.2 %shard_map.130 = (f32[8,128,128]{2,1,0:T(8,128)}, f32[8,128,128]{2,1,0:T(8,128)}, f32[8,128,128]{2,1,0:T(8,128)}, f32[8,128,128]{2,1,0:T(8,128)}) custom-call(f32[4,8]{1,0:T(4,128)S(1)} %copy-done.8, f32[63,176,128]{2,1,0:T(8,128)S(1)} %shard_map.129.T, f32[7,128,128]{2,1,0:T(8,128)S(1)} %copy-done.5), custom_call_target="tpu_custom_call" | custom-call | tf_op jit(solution)/shard_map/pallas_call | solution.py:490
Async XLA Ops:
  0.6 40.8 %copy-start.8 = (f32[4,8]{1,0:T(4,128)S(1)}, f32[4,8]{1,0:T(4,128)}, u32[]{:S(2)}) copy-start(f32[4,8]{1,0:T(4,128)} %coef.1) | copy-start | bytes 388
  3.3 1.0 %copy-start = (f32[8,128,128]{2,1,0:T(8,128)S(1)}, f32[8,128,128]{2,1,0:T(8,128)}, u32[]{:S(2)}) copy-start(f32[8,128,128]{2,1,0:T(8,128)} %t.1) | copy-start | bytes 1572868
  4.3 1.0 %copy-start.1 = (f32[8,128,128]{2,1,0:T(8,128)S(1)}, f32[8,128,128]{2,1,0:T(8,128)}, u32[]{:S(2)}) copy-start(f32[8,128,128]{2,1,0:T(8,128)} %s.1) | copy-start | bytes 1572868
  5.3 1.0 %copy-start.2 = (f32[8,128,128]{2,1,0:T(8,128)S(1)}, f32[8,128,128]{2,1,0:T(8,128)}, u32[]{:S(2)}) copy-start(f32[8,128,128]{2,1,0:T(8,128)} %u.1) | copy-start | bytes 1572868
  6.4 1.0 %copy-start.3 = (f32[8,128,128]{2,1,0:T(8,128)S(1)}, f32[8,128,128]{2,1,0:T(8,128)}, u32[]{:S(2)}) copy-start(f32[8,128,128]{2,1,0:T(8,128)} %v.1) | copy-start | bytes 1572868
  7.4 1.0 %copy-start.4 = (s32[8,128,128]{2,1,0:T(8,128)S(1)}, s32[8,128,128]{2,1,0:T(8,128)}, u32[]{:S(2)}) copy-start(s32[8,128,128]{2,1,0:T(8,128)} %wet.1) | copy-start | bytes 1572868
  8.5 0.8 %copy-start.6 = (f32[128,128]{1,0:T(8,128)S(1)}, f32[128,128]{1,0:T(8,128)}, u32[]{:S(2)}) copy-start(f32[128,128]{1,0:T(8,128)} %mx.1) | copy-start | bytes 196612
  9.3 0.8 %copy-start.7 = (f32[128,128]{1,0:T(8,128)S(1)}, f32[128,128]{1,0:T(8,128)}, u32[]{:S(2)}) copy-start(f32[128,128]{1,0:T(8,128)} %my.1) | copy-start | bytes 196612
  10.1 31.3 %copy-start.5 = (f32[7,128,128]{2,1,0:T(8,128)S(1)}, f32[7,128,128]{2,1,0:T(8,128)}, u32[]{:S(2)}) copy-start(f32[7,128,128]{2,1,0:T(8,128)} %idf.1) | copy-start | bytes 1376260
